TPU v7x, 256 devices: a whole 4x4x8 slice. The times are simulated.
256 devices in a mesh: gx: 16 (over x, z_lo), gy: 16 (over y, z_hi, core).
Axes of the slice: x: 4, y: 4, z: 8 (z_hi: 2, z_lo: 4; z = z_hi * 4 + z_lo), core: 2. Of those that a mesh axis runs over, the one named last changes fastest.
Arguments:
- images: float32 [1024, 128, 2048], P(None, 'gx', 'gy'), may hold values from 0 to 600, as said below
Outputs:
- colocal: float32 [1024, 1024], P(('gx', 'gy'))
Inputs may be any that keep to these rules, and one draw needn't show every extreme that they name: `images`: intensities are non-negative.
All inputs are finite; a program needn't handle non-finite values.
Results may differ from a plain program's by a relative error of at most 0.00035.
Values sent between devices are 32-bit elements; how exact they have to be, the bound alone decides.
No kernel may reach another device: no remote copies, remote signals or barrier semaphores. Data moves between devices by JAX's collectives and lax.ppermute only.
A program may use at most 128 MiB of HBM per device.

v0:
```python
import math

import jax
import jax.numpy as jnp
from jax import lax
from jax.sharding import PartitionSpec as P

sigma_sq = 2.25


def extended(array, sides, width):
    for axis, dim in sides:
        peers, length = (lax.axis_size(axis), array.shape[dim])
        up = [(i, (i + 1) % peers) for i in range(peers - 1)]
        down = [(j, i) for i, j in up]
        last = lax.slice_in_dim(array, length - width, length, axis=dim)
        initial = lax.slice_in_dim(array, 0, width, axis=dim)
        before = lax.ppermute(last, axis, up)
        after = lax.ppermute(initial, axis, down)
        array = jnp.concatenate([before, array, after], axis=dim)
    return array


def stencil_taps():
    raw = [math.exp(-k * k / (2.0 * sigma_sq)) for k in range(-4, 5)]
    total = sum(raw)
    return [value / total for value in raw]


def smooth_along(padded, along, length):
    taps = stencil_taps()
    result = taps[0] * lax.slice_in_dim(padded, 0, length, axis=along)
    for k in range(1, 9):
        result = result + taps[k] * lax.slice_in_dim(padded, k, k + length, axis=along)
    return result


def local(images):
    count_images = images.shape[0]
    tile_rows = images.shape[1]
    tile_cols = images.shape[2]
    padded = extended(images, (("gx", 1),), 4)
    vertical = smooth_along(padded, 1, tile_rows)
    widened = extended(vertical, (("gy", 2),), 4)
    smooth = smooth_along(widened, 2, tile_cols)
    pixel_count = jnp.float32(tile_rows * tile_cols * lax.axis_size("gx") * lax.axis_size("gy"))
    total = lax.psum(jnp.sum(smooth, axis=(1, 2)), ("gx", "gy"))
    mean = total / pixel_count
    centered = smooth - mean[:, None, None]
    spread = lax.psum(jnp.sum(centered * centered, axis=(1, 2)), ("gx", "gy"))
    scale = 1.0 / jnp.sqrt(spread + 1e-06)
    unit = (centered * scale[:, None, None]).astype(jnp.bfloat16).reshape(count_images, -1)
    return lax.psum_scatter(
        lax.dot_general(unit, unit, (((1,), (1,)), ((), ())), preferred_element_type=jnp.float32),
        ("gx", "gy"),
        scatter_dimension=0,
        tiled=True,
    )


def solution(mesh):
    return jax.shard_map(
        local,
        mesh=mesh,
        in_specs=(P(None, "gx", "gy"),),
        out_specs=P(("gx", "gy"), None),
        check_vma=False,
    )
```

profile of v0, /device:TPU:32, one launch (start us, length us, event | category | flops | bytes accessed | tf_op | source)
XLA Modules:
  0.0 591.4 jit_solution(8394284555404207164)
XLA Ops:
  6.5 0.0 all-reduce.3.cloned.1.call-start
  6.5 4.2 fusion.49
  10.7 0.1 copy.16
  10.9 3.8 collective-permute-start.1
  14.6 1.5 copy.15
  16.2 2.1 collective-permute-start
  18.2 5.5 copy.6
  23.7 36.7 %collective-permute-done.1 = f32[1024,4,128]{2,0,1:T(8,128)} collective-permute-done((f32[1024,4,128]{2,0,1:T(8,128)S(1)}, f32[1024,4,128]{2,0,1:T(8,128)}, u32[]{:S(2)}, u32[]{:S(2)}) %collective-permute-start.1) | collective-permute-done | bytes 2097184 | tf_op jit(solution)/shard_map/ppermute | solution.py:19
  60.4 2.4 copy.10
  62.8 1.1 collective-permute-done
  63.9 3.1 copy.5
  67.0 24.7 %fusion.23 = f32[1024,8,128]{0,1,2:T(8,128)S(1)} fusion(f32[1024,8,128]{0,1,2:T(8,128)} %copy.6, f32[1024,4,128]{0,1,2:T(4,128)S(1)} %copy.10, f32[1024,4,128]{0,1,2:T(4,128)} %copy.5), kind=kLoop, calls=%fused_computation.41 | loop fusion | flops 26214400 | bytes 12582912 | tf_op jit(solution)/shard_map/add | solution.py:34
  91.7 1.3 collective-permute-start.2
  93.0 1.3 collective-permute-start.3
  94.3 0.0 collective-permute-done.2
  94.3 9.2 %collective-permute-done.3 = f32[1024,8,4]{0,1,2:T(8,128)S(1)} collective-permute-done((f32[1024,8,4]{0,1,2:T(8,128)S(1)}, f32[1024,8,4]{0,1,2:T(8,128)S(1)}, u32[]{:S(2)}, u32[]{:S(2)}) %collective-permute-start.3) | collective-permute-done | bytes 131104 | tf_op jit(solution)/shard_map/ppermute | solution.py:19
  103.5 6.0 %fusion.46 = (f32[1024]{0:T(1024)S(1)}, f32[1024,8,128]{0,1,2:T(8,128)}) fusion(f32[1024,8,4]{0,1,2:T(8,128)S(1)} %collective-permute-done.3, f32[1024,8,128]{0,1,2:T(8,128)S(1)} %fusion.23, f32[1024,8,4]{0,1,2:T(8,128)S(1)} %collective-permute-done.2), kind=kLoop, calls=%fused_computation.76 | loop fusion | flops 27261952 | bytes 8654848 | tf_op jit(solution)/shard_map/reduce_sum | solution.py:47
  109.5 126.9 %psum.14 = f32[1024]{0:T(1024)S(1)} all-reduce(f32[1024]{0:T(1024)S(1)} %get-tuple-element.5), channel_id=1, replica_groups=mesh['gx'=16,'gy'=16] {'gx','gy'}, use_global_device_ids=true, to_apply=%region_1.0 | all-reduce | flops 1024 | bytes 8192 | tf_op jit(solution)/shard_map/psum | solution.py:47
  236.4 2.7 multiply_reduce_fusion
  239.0 74.4 %psum.15 = f32[1024]{0:T(1024)S(1)} all-reduce(f32[1024]{0:T(1024)S(1)} %multiply_reduce_fusion), channel_id=1, replica_groups=mesh['gx'=16,'gy'=16] {'gx','gy'}, use_global_device_ids=true, to_apply=%region_3.0 | all-reduce | flops 1024 | bytes 8192 | tf_op jit(solution)/shard_map/psum | solution.py:50
  313.4 7.8 %convolution_bitcast_fusion = f32[1024,1024]{1,0:T(8,128)} fusion(f32[1024,8,128]{0,1,2:T(8,128)} %get-tuple-element.6, f32[1024]{0:T(1024)S(1)} %add_rsqrt_fusion, f32[1024]{0:T(1024)S(1)} %broadcast_multiply_fusion), kind=kOutput, calls=%fused_computation.70 | convolution fusion | flops 2150629376 | bytes 8396800 | tf_op jit(solution)/shard_map/dot_general | solution.py:54
  321.2 0.0 all-reduce.3.cloned.1.call-update
  321.2 261.9 %all-reduce.3.cloned.1.call-done = f32[1024,1024]{1,0:T(8,128)} async-done(((f32[1024,1024]{1,0:T(8,128)}), f32[1024,1024]{1,0:T(8,128)}) %all-reduce.3.cloned.1.call-update) | async-done | bytes 4194320
  583.1 1.4 constant_dynamic-slice_fusion
  (3 shorter events, 0.0 us)
Async XLA Ops:
  6.5 576.6 %all-reduce.3.cloned.1.call-start = ((), (), s32[]{:S(2)}) async-start(), calls=%async_computation | async-start | bytes 8388608
  10.9 49.6 %collective-permute-start.1 = (f32[1024,4,128]{2,0,1:T(8,128)S(1)}, f32[1024,4,128]{2,0,1:T(8,128)}, u32[]{:S(2)}, u32[]{:S(2)}) collective-permute-start(f32[1024,4,128]{2,0,1:T(8,128)S(1)} %copy.16), channel_id=1, source_target_pairs={{16,0},{32,16},{48,32},{64,48},{80,64},{96,80},{112,96},{128,112},... | collective-permute-start | bytes 6291464 | tf_op jit(solution)/shard_map/ppermute | solution.py:19
  16.2 47.7 %collective-permute-start = (f32[1024,4,128]{2,0,1:T(8,128)}, f32[1024,4,128]{2,0,1:T(8,128)}, u32[]{:S(2)}, u32[]{:S(2)}) collective-permute-start(f32[1024,4,128]{2,0,1:T(8,128)} %copy.15), channel_id=1, source_target_pairs={{0,16},{16,32},{32,48},{48,64},{64,80},{80,96},{96,112},{112,128},... | collective-permute-start | bytes 6291464 | tf_op jit(solution)/shard_map/ppermute | solution.py:18
  91.7 2.6 collective-permute-start.2
  93.0 10.5 %collective-permute-start.3 = (f32[1024,8,4]{0,1,2:T(8,128)S(1)}, f32[1024,8,4]{0,1,2:T(8,128)S(1)}, u32[]{:S(2)}, u32[]{:S(2)}) collective-permute-start(f32[1024,8,4]{0,1,2:T(8,128)S(1)} %get-tuple-element.8), channel_id=1, source_target_pairs={{1,0},{2,1},{3,2},{4,3},{5,4},{6,5},{7,6},{8,7},{9,8},{10,9},{11,1... | collective-permute-start | bytes 393224 | tf_op jit(solution)/shard_map/ppermute | solution.py:19
Sparse Core Ops, SparseCore 0:
  321.4 261.7 all-reduce.2
where the time goes:
time: 595 us; the launch traced here: 591 us
  waiting for transfers between devices  309 us (52%)
  blocking collectives  201 us (34%)
  other arithmetic  33.3 us (6%)
  local copies, waits for them, and re-layouts  18.2 us (3%)
  between operations  13.5 us (2%)
  starting transfers between devices  8.42 us (1%)
  matrix products  7.84 us (1%)
    unnamed x2, waiting for transfers between devices  262 us
    psum x1, blocking collectives, local(): total = lax.psum(jnp.sum(smooth, axis=(1, 2)), ('gx', 'gy'))  127 us
    psum x1, blocking collectives, local(): spread = lax.psum(jnp.sum(centered * centered, axis=(1, 2)), ('gx', 'gy'))  74.4 us
    ppermute x2, waiting for transfers between devices, extended(): after = lax.ppermute(initial, axis, down)  45.9 us
    add x1, other arithmetic, smooth_along(): result + taps[k] * lax.slice_in_dim(padded, k, k + length, axis=along)  24.7 us
  transfers between devices with their start and end apart: 5, of which 4 were waited for; matrix products, arithmetic and copies ran while one was open for 2% of the time, Pallas kernels for 0%

commit v1 on v0

v1 whole, which is shorter than its diff:
```python
import functools
import math

import jax
import jax.numpy as jnp
from jax import lax
from jax.experimental import pallas as pl
from jax.experimental.pallas import tpu as pltpu
from jax.sharding import Mesh, PartitionSpec as P

f32 = jnp.float32
HI = lax.Precision.HIGHEST
NT = (((1,), (1,)), ((), ()))
TILE = 8 * 128
GX, GY = ("x", "zl"), ("y", "zh", "c")
AXES = GX + GY


def stencil_taps():
    raw = [math.exp(-k * k / 4.5) for k in range(-4, 5)]
    total = sum(raw)
    return [value / total for value in raw]


TAPS = stencil_taps()


def survey(x_ref, left_ref, right_ref):
    lane = lax.broadcasted_iota(jnp.int32, (64, 128), 1)
    left = jnp.zeros((64, 128), f32)
    right = jnp.zeros((64, 128), f32)
    for g in range(4):
        for r in range(8):
            row = x_ref[g, pl.ds(r, 64, stride=8), :]
            slot = g * 32 + r * 4
            here = (lane >= slot) & (lane < slot + 4)
            left = jnp.where(here, pltpu.roll(row, slot, 1) if slot else row, left)
            right = jnp.where(here, pltpu.roll(row, (slot + 4) % 128, 1), right)
    left_ref[...] = left
    right_ref[...] = right


def row_pass(first_group, x_ref, left_ref, right_ref, order_ref, top_ref, bot_ref):
    turn = 128 - 32 * (first_group + pl.program_id(0))
    lane = lax.broadcasted_iota(jnp.int32, (8, 128), 1)

    def step(s, carry):
        at = pl.ds(pl.multiple_of(s * 8, 8), 8)
        left = pltpu.roll(left_ref[at, :], turn, 1)
        right = pltpu.roll(right_ref[at, :], turn, 1)
        for r in range(8):
            row = x_ref[0, pl.ds(s * 64 + r, 8, stride=8), :]
            ends = jnp.where(
                lane < 64,
                pltpu.roll(right, 128 - 4 * r, 1) if r else right,
                pltpu.roll(left, 124 - 4 * r, 1),
            )
            smooth = row * TAPS[4]
            for k in range(1, 5):
                after = pltpu.roll(jnp.where(lane < k, ends, row), 128 - k, 1)
                before = pltpu.roll(jnp.where(lane >= 128 - k, ends, row), k, 1)
                smooth = smooth + (after + before) * TAPS[4 + k]
            if r < 4:
                top_ref[r, at, :] = smooth
            else:
                bot_ref[r - 4, at, :] = smooth
        return carry

    lax.fori_loop(0, 16, step, 0)


def column_pass(above_ref, below_ref, top_ref, bot_ref, u_ref, spread_ref, mean_ref, square_ref, level_ref):
    def step(s, carry):
        at = pl.ds(pl.multiple_of(s * 16, 16), 16)
        rows = [ref[i, at, :] for ref in (above_ref, top_ref, bot_ref, below_ref) for i in range(4)]
        smooth = []
        for r in range(8):
            v = rows[r + 4] * TAPS[4]
            for k in range(1, 5):
                v = v + (rows[r + 4 - k] + rows[r + 4 + k]) * TAPS[4 + k]
            smooth.append(v)
        total = ((smooth[0] + smooth[1]) + (smooth[2] + smooth[3])) + ((smooth[4] + smooth[5]) + (smooth[6] + smooth[7]))
        mean = jnp.sum(total, axis=1, keepdims=True) * f32(1.0 / TILE)
        acc = jnp.zeros((16, 128), f32)
        for r in range(8):
            centered = smooth[r] - mean
            acc = acc + centered * centered
            u_ref[at, r * 128:(r + 1) * 128] = centered.astype(jnp.bfloat16)
        square_ref[at, :] = acc
        level_ref[at, :] = jnp.broadcast_to(mean, (16, 128))
        return carry

    lax.fori_loop(0, 8, step, 0)
    ones = jnp.ones((8, 128), f32)
    pick = jnp.where(lax.broadcasted_iota(jnp.int32, (8, 128), 1) == 0, f32(1), f32(0))
    spread_ref[...] = lax.dot_general(ones, square_ref[...], NT, precision=HI, preferred_element_type=f32)[0:1]
    mean_ref[...] = lax.dot_general(pick, level_ref[...], NT, precision=HI, preferred_element_type=f32)[0:1]


def gram(u0_ref, u1_ref, spread_ref, mean_ref, keep_ref, send_ref):
    first = lax.axis_index("c") == 0
    x = pl.program_id(0)
    at = pl.ds(pl.multiple_of((x % 2) * 256, 256), 256)
    rows = jnp.where(x < 2, u0_ref[at, :], u1_ref[at, :])
    part = jnp.concatenate(
        [lax.dot_general(rows, u[...], NT, preferred_element_type=f32) for u in (u0_ref, u1_ref)], axis=1
    )
    sub = lax.broadcasted_iota(jnp.int32, (8, 128), 0)
    for zl in range(4):
        for y in range(4):
            at = (zl * 4 + y) * 16
            for cb in range(8):
                a = part[at:at + 8, cb * 128:(cb + 1) * 128]
                b = part[at + 8:at + 16, cb * 128:(cb + 1) * 128]
                c0 = jnp.where(sub < 4, a, pltpu.roll(b, 4, 0))
                c1 = jnp.where(sub < 4, pltpu.roll(a, 4, 0), b)
                keep_ref[y, zl * 8 + cb] = jnp.where(first, c0, c1)
                send_ref[y, zl * 8 + cb] = jnp.where(first, c1, c0)
    for y in range(4):
        for ref, own, other in ((keep_ref, 33, 34), (send_ref, 34, 33)):
            ref[y, 32] = spread_ref[...]
            ref[y, own] = mean_ref[...]
            ref[y, other] = jnp.zeros((8, 128), f32)


def between(shift_ref, select):
    wide = jnp.concatenate([shift_ref[cb] for cb in range(8)], axis=1)
    rows = [
        lax.dot_general(one_hot, shift_ref[block], NT, precision=HI, preferred_element_type=f32)
        for block, one_hot in select
    ]
    rows = jnp.concatenate(rows, axis=0) if len(rows) > 1 else rows[0]
    return jnp.dot(rows, wide, precision=HI, preferred_element_type=f32)


def fold(part_ref, out_ref, shift_ref):
    x, y, c = lax.axis_index("x"), lax.axis_index("y"), lax.axis_index("c")
    sub = lax.broadcasted_iota(jnp.int32, (8, 128), 0)
    lane = lax.broadcasted_iota(jnp.int32, (8, 128), 1)

    def summed(t):
        s = part_ref[0, t]
        for p in range(1, 16):
            s = s + part_ref[p, t]
        return s

    mean = (summed(33) + summed(34)) * f32(1.0 / 32)
    spread = summed(32)
    for k in range(2):
        for p in range(16):
            shift = part_ref[p, 33 + k] - mean
            spread = spread + shift * shift * f32(TILE)
            for cb in range(8):
                shift_ref[cb, k * 16 + p:k * 16 + p + 1, :] = shift[cb:cb + 1]
    select = []
    for zl in range(4):
        want = (zl % 2) * 64 + y * 16 + (sub // 4) * 8 + c * 4 + sub % 4
        select.append((2 * x + zl // 2, jnp.where(lane == want, f32(1), f32(0))))
    extra = between(shift_ref, select) * f32(TILE)
    for zl in range(4):
        for k in range(4):
            a, b = [
                summed(zl * 8 + cb) + extra[zl * 8:zl * 8 + 8, cb * 128:(cb + 1) * 128] for cb in (2 * k, 2 * k + 1)
            ]
            out_ref[zl * 2, k] = jnp.where(sub < 4, a, pltpu.roll(b, 4, 0))
            out_ref[zl * 2 + 1, k] = jnp.where(sub < 4, pltpu.roll(a, 4, 0), b)
        for zh in range(2):
            out_ref[zl * 2 + zh, 4] = spread
            out_ref[zl * 2 + zh, 5] = mean


def finish(part_ref, out_ref, shift_ref):
    first_row = lax.axis_index(AXES) * 4
    sub = lax.broadcasted_iota(jnp.int32, (8, 128), 0)
    lane = lax.broadcasted_iota(jnp.int32, (8, 128), 1)

    def summed(t):
        s = part_ref[0, t]
        for p in range(1, 8):
            s = s + part_ref[p, t]
        return s

    mean = summed(5) * f32(1.0 / 8)
    spread = summed(4)
    for p in range(8):
        shift = part_ref[p, 5] - mean
        spread = spread + shift * shift * f32(32 * TILE)
        for cb in range(8):
            shift_ref[cb, p:p + 1, :] = shift[cb:cb + 1]
    one_hot = jnp.where(lane == first_row % 128 + sub % 4, f32(1), f32(0))
    extra = between(shift_ref, [(first_row // 128, one_hot)]) * f32(32 * TILE)
    scale = 1.0 / jnp.sqrt(spread + 1e-06)
    flat = sub * 128 + lane
    own = jnp.zeros((8, 128), f32)
    for i in range(4):
        value = jnp.sum(jnp.where(flat == first_row + i, scale, 0.0))
        own = jnp.where((sub & 3) == i, value, own)
    for k in range(4):
        at, to = 2 * k * 128, (2 * k + 1) * 128
        cols = jnp.where(sub < 4, scale[2 * k:2 * k + 1, :], scale[2 * k + 1:2 * k + 2, :])
        more = jnp.where(sub < 4, extra[:, at:to], extra[:, to:to + 128])
        tile = (summed(k) + more) * cols * own
        out_ref[:, at:to] = tile[0:4]
        out_ref[:, to:to + 128] = tile[4:8]


def local(images):
    shape = jax.ShapeDtypeStruct
    vmem = pl.BlockSpec(memory_space=pltpu.VMEM)
    params = pltpu.CompilerParams(vmem_limit_bytes=48 * 1024 * 1024)
    grouped = images.reshape(4, 2048, 128)
    up = [(i, i + 1) for i in range(15)]
    down = [(j, i) for i, j in up]

    strip = pl.BlockSpec((64, 128), lambda i: (i, 0))
    left, right = pl.pallas_call(
        survey,
        grid=(4,),
        in_specs=[pl.BlockSpec((4, 512, 128), lambda i: (0, i, 0))],
        out_specs=[strip, strip],
        out_shape=[shape((256, 128), f32)] * 2,
        compiler_params=params,
    )(grouped)
    from_left = lax.ppermute(right, GY, up)
    from_right = lax.ppermute(left, GY, down)

    halves, ghosts = [], []
    strip = pl.BlockSpec((128, 128), lambda g, i: (i, 0))
    rows = pl.BlockSpec((4, 128, 128), lambda g, i: (0, 2 * g + i, 0))
    for q in range(2):
        top, bot = pl.pallas_call(
            functools.partial(row_pass, 2 * q),
            grid=(2, 2),
            in_specs=[
                pl.BlockSpec((1, 1024, 128), lambda g, i, q=q: (2 * q + g, i, 0)),
                strip,
                strip,
                pl.BlockSpec(memory_space=pl.ANY),
            ],
            out_specs=[rows, rows],
            out_shape=[shape((4, 512, 128), f32)] * 2,
            compiler_params=params,
        )(grouped, from_left, from_right, halves[-1][0] if q else from_left)
        halves.append((top, bot))
        ghosts.append((lax.ppermute(bot, GX, up), lax.ppermute(top, GX, down)))

    units, spreads, means = [], [], []
    rows = pl.BlockSpec((4, 128, 128), lambda i: (0, i, 0))
    line = pl.BlockSpec((1, 128), lambda i: (0, i))
    for q in range(2):
        unit, spread, mean = pl.pallas_call(
            column_pass,
            grid=(4,),
            in_specs=[rows] * 4,
            out_specs=[pl.BlockSpec((128, 1024), lambda i: (i, 0)), line, line],
            out_shape=[shape((512, 1024), jnp.bfloat16), shape((1, 512), f32), shape((1, 512), f32)],
            scratch_shapes=[pltpu.VMEM((128, 128), f32)] * 2,
            compiler_params=params,
        )(*ghosts[q], *halves[q])
        units.append(unit)
        spreads.append(spread)
        means.append(mean)
    spread = jnp.concatenate(spreads, axis=1).reshape(8, 128)
    mean = jnp.concatenate(means, axis=1).reshape(8, 128)

    block = pl.BlockSpec((4, 35, 8, 128), lambda i: (i, 0, 0, 0))
    unit = pl.BlockSpec((512, 1024), lambda i: (0, 0))
    tile = pl.BlockSpec((8, 128), lambda i: (0, 0))
    keep, send = pl.pallas_call(
        gram,
        grid=(4,),
        in_specs=[unit, unit, tile, tile],
        out_specs=[block, block],
        out_shape=[shape((16, 35, 8, 128), f32)] * 2,
        compiler_params=params,
    )(*units, spread, mean)

    part = keep + lax.ppermute(send, "c", [(0, 1), (1, 0)])
    part = lax.all_to_all(part, ("x", "y"), 0, 0, tiled=True)
    part = pl.pallas_call(
        fold,
        in_specs=[vmem],
        out_specs=vmem,
        out_shape=shape((8, 6, 8, 128), f32),
        scratch_shapes=[pltpu.VMEM((8, 32, 128), f32)],
        compiler_params=params,
    )(part)
    part = lax.all_to_all(part, ("zl", "zh"), 0, 0, tiled=True)
    return pl.pallas_call(
        finish,
        in_specs=[vmem],
        out_specs=vmem,
        out_shape=shape((4, 1024), f32),
        scratch_shapes=[pltpu.VMEM((8, 8, 128), f32)],
        compiler_params=params,
    )(part)


def solution(mesh):
    fine = Mesh(mesh.devices.reshape(4, 4, 4, 2, 2), AXES)
    return jax.shard_map(
        local,
        mesh=fine,
        in_specs=(P(None, GX, GY),),
        out_specs=P(AXES, None),
        check_vma=False,
    )
```

time: 595 us -> 204 us (0.34)
  waiting for transfers between devices: 309 us -> 73.8 us
  blocking collectives: 201 us -> 55 us
  Pallas kernels: 0 us -> 57 us
  other arithmetic: 33.3 us -> 0.36 us
  local copies, waits for them, and re-layouts: 18.2 us -> 2.19 us
  between operations: 13.5 us -> 0.11 us
  matrix products: 7.84 us -> 0 us
  starting transfers between devices: 8.42 us -> 15 us
    unnamed x2 -> x0, waiting for transfers between devices: 262 us -> none
    psum x2 -> x0, blocking collectives: 201 us -> none  [the longest x1 127 us: local(): total = lax.psum(jnp.sum(smooth, axis=(1, 2)), ('gx', 'gy'))]
    pallas_call x0 -> x8, Pallas kernels: none -> 57 us  [the longest x2 37.7 us: local(): pl.pallas_call(functools.partial(row_pass, 2 * q), grid=(2, 2), in_specs=...]
    all_to_all x0 -> x2, blocking collectives: none -> 55 us  [the longest x1 38.9 us: local(): part = lax.all_to_all(part, ('x', 'y'), 0, 0, tiled=True)]
    ppermute x4 -> x7, waiting for transfers between devices: 47 us -> 73.8 us  [the longest x4 61.3 us: local(): ghosts.append((lax.ppermute(bot, GX, up), lax.ppermute(top, GX, down)))]
    add x1, other arithmetic: 24.7 us -> 0.34 us  [local(): part = keep + lax.ppermute(send, 'c', [(0, 1), (1, 0)])]
    reduce_sum x2 -> x0, other arithmetic: 8.68 us -> none  [the longest x1 6.01 us: local(): total = lax.psum(jnp.sum(smooth, axis=(1, 2)), ('gx', 'gy'))]
    dot_general x1 -> x0, matrix products: 7.84 us -> none  [local(): lax.dot_general(unit, unit, (((1,), (1,)), ((), ())), preferred_element_t...]
  transfers between devices with their start and end apart: 5 -> 7, of which waited for: 4 -> 4; matrix products, arithmetic and copies ran while one was open for 2% -> 0% of each run, Pallas kernels for 0% -> 12%
where the time goes in v1:
time: 204 us; the launch traced here: 203 us
  waiting for transfers between devices  73.8 us (36%)
  Pallas kernels  57 us (28%)
  blocking collectives  55 us (27%)
  starting transfers between devices  15 us (7%)
  local copies, waits for them, and re-layouts  2.19 us (1%)
    ppermute x4, waiting for transfers between devices, local(): ghosts.append((lax.ppermute(bot, GX, up), lax.ppermute(top, GX, down)))  61.3 us
    all_to_all x1, blocking collectives, local(): part = lax.all_to_all(part, ('x', 'y'), 0, 0, tiled=True)  38.9 us
    pallas_call x2, Pallas kernels, local(): pl.pallas_call(functools.partial(row_pass, 2 * q), grid=(2, 2), in_specs=...  37.7 us
    all_to_all x1, blocking collectives, local(): part = lax.all_to_all(part, ('zl', 'zh'), 0, 0, tiled=True)  16.1 us
    ppermute x4, starting transfers between devices, local(): ghosts.append((lax.ppermute(bot, GX, up), lax.ppermute(top, GX, down)))  11.8 us
    pallas_call x2, Pallas kernels, local(): pl.pallas_call(column_pass, grid=(4,), in_specs=[rows] * 4, out_specs=[pl...  11.1 us
    ppermute x1, waiting for transfers between devices, local(): from_right = lax.ppermute(left, GY, down)  8 us
    ppermute x1, waiting for transfers between devices, local(): part = keep + lax.ppermute(send, 'c', [(0, 1), (1, 0)])  4.54 us
  transfers between devices with their start and end apart: 7, of which 4 were waited for; matrix products, arithmetic and copies ran while one was open for 0% of the time, Pallas kernels for 12%

profile of v1, /device:TPU:32, one launch (start us, length us, event | category | flops | bytes accessed | tf_op | source)
XLA Modules:
  0.0 203.4 jit_solution(17863721361449138638)
XLA Ops:
  0.0 0.0 copy-start
  0.0 2.2 %copy-done = f32[1024,8,128]{2,1,0:T(8,128)S(1)} copy-done((f32[1024,8,128]{2,1,0:T(8,128)S(1)}, f32[1024,8,128]{2,1,0:T(8,128)}, u32[]{:S(2)}) %copy-start) | copy-done | bytes 4194328
  2.2 2.8 %shard_map.17 = (f32[256,128]{1,0:T(8,128)S(1)}, f32[256,128]{1,0:T(8,128)S(1)}) custom-call(f32[4,2048,128]{2,1,0:T(8,128)S(1)} %bitcast.5), custom_call_target="tpu_custom_call" | custom-call | tf_op jit(solution)/shard_map/pallas_call | solution.py:216
  5.0 1.7 collective-permute-start
  6.8 1.3 collective-permute-start.1
  8.1 0.0 collective-permute-done.left_ref.order_ref
  8.1 8.0 %collective-permute-done.1.right_ref = f32[256,128]{1,0:T(8,128)S(1)} collective-permute-done((f32[256,128]{1,0:T(8,128)S(1)}, f32[256,128]{1,0:T(8,128)S(1)}, u32[]{:S(2)}, u32[]{:S(2)}) %collective-permute-start.1) | collective-permute-done | bytes 131104 | tf_op jit(solution)/shard_map/ppermute | solution.py:225
  16.1 18.8 %shard_map.18 = (f32[4,512,128]{2,1,0:T(8,128)S(1)}, f32[4,512,128]{2,1,0:T(8,128)S(1)}) custom-call(f32[4,2048,128]{2,1,0:T(8,128)} %bitcast.3, f32[256,128]{1,0:T(8,128)S(1)} %collective-permute-done.left_ref.order_ref, f32[256,128]{1,0:T(8,128)S(1)} %collective-permute-done.1.right_ref, f32[256,128]{1,0:T(8,128)S(1)} %collective-permute-done.left_ref.order_ref), custom_call_target="tpu_custom_call" | custom-call | tf_op jit(solution)/shard_map/pallas_call | solution.py:231
  34.9 2.9 %collective-permute-start.2 = (f32[4,512,128]{2,1,0:T(8,128)S(1)}, f32[4,512,128]{2,1,0:T(8,128)S(1)}, u32[]{:S(2)}, u32[]{:S(2)}) collective-permute-start(f32[4,512,128]{2,1,0:T(8,128)S(1)} %get-tuple-element.21.bot_ref), channel_id=1, source_target_pairs={{0,16},{16,32},{32,48},{48,64},{64,80},{80,96},{96,112},{112,128},... | collective-permute-start | bytes 3145736 | tf_op jit(solution)/shard_map/ppermute | solution.py:245
  37.8 3.0 %collective-permute-start.3 = (f32[4,512,128]{2,1,0:T(8,128)S(1)}, f32[4,512,128]{2,1,0:T(8,128)S(1)}, u32[]{:S(2)}, u32[]{:S(2)}) collective-permute-start(f32[4,512,128]{2,1,0:T(8,128)S(1)} %get-tuple-element.22.top_ref.order_ref), channel_id=1, source_target_pairs={{16,0},{32,16},{48,32},{64,48},{80,64},{96,80},{112,96},{128,112},... | collective-permute-start | bytes 3145736 | tf_op jit(solution)/shard_map/ppermute | solution.py:245
  40.8 18.9 %shard_map.20 = (f32[4,512,128]{2,1,0:T(8,128)S(1)}, f32[4,512,128]{2,1,0:T(8,128)S(1)}) custom-call(f32[4,2048,128]{2,1,0:T(8,128)} %bitcast.4, f32[256,128]{1,0:T(8,128)S(1)} %collective-permute-done.left_ref.order_ref, f32[256,128]{1,0:T(8,128)S(1)} %collective-permute-done.1.right_ref, f32[4,512,128]{2,1,0:T(8,128)S(1)} %get-tuple-element.22.top_ref.order_ref), custom_call_target="tpu_custom_call" | custom-call | tf_op jit(solution)/shard_map/pallas_call | solution.py:231
  59.7 2.9 %collective-permute-start.4 = (f32[4,512,128]{2,1,0:T(8,128)S(1)}, f32[4,512,128]{2,1,0:T(8,128)S(1)}, u32[]{:S(2)}, u32[]{:S(2)}) collective-permute-start(f32[4,512,128]{2,1,0:T(8,128)S(1)} %get-tuple-element.24.bot_ref), channel_id=1, source_target_pairs={{0,16},{16,32},{32,48},{48,64},{64,80},{80,96},{96,112},{112,128},... | collective-permute-start | bytes 3145736 | tf_op jit(solution)/shard_map/ppermute | solution.py:245
  62.5 3.0 %collective-permute-start.5 = (f32[4,512,128]{2,1,0:T(8,128)S(1)}, f32[4,512,128]{2,1,0:T(8,128)S(1)}, u32[]{:S(2)}, u32[]{:S(2)}) collective-permute-start(f32[4,512,128]{2,1,0:T(8,128)S(1)} %get-tuple-element.25.top_ref), channel_id=1, source_target_pairs={{16,0},{32,16},{48,32},{64,48},{80,64},{96,80},{112,96},{128,112},... | collective-permute-start | bytes 3145736 | tf_op jit(solution)/shard_map/ppermute | solution.py:245
  65.6 0.0 collective-permute-done.2.above_ref
  65.6 28.3 %collective-permute-done.3.below_ref = f32[4,512,128]{2,1,0:T(8,128)S(1)} collective-permute-done((f32[4,512,128]{2,1,0:T(8,128)S(1)}, f32[4,512,128]{2,1,0:T(8,128)S(1)}, u32[]{:S(2)}, u32[]{:S(2)}) %collective-permute-start.3) | collective-permute-done | bytes 1048608 | tf_op jit(solution)/shard_map/ppermute | solution.py:245
  93.9 5.5 %shard_map.19 = (bf16[512,1024]{1,0:T(8,128)(2,1)S(1)}, f32[1,512]{1,0:T(1,128)S(1)}, f32[1,512]{1,0:T(1,128)S(1)}) custom-call(f32[4,512,128]{2,1,0:T(8,128)S(1)} %collective-permute-done.2.above_ref, f32[4,512,128]{2,1,0:T(8,128)S(1)} %collective-permute-done.3.below_ref, f32[4,512,128]{2,1,0:T(8,128)S(1)} %get-tuple-element.22.top_ref.order_ref, ...), custom_call_target="tpu_custom_call" | custom-call | tf_op jit(solution)/shard_map/pallas_call | solution.py:251
  99.4 0.0 collective-permute-done.4.above_ref
  99.4 33.0 %collective-permute-done.5.below_ref = f32[4,512,128]{2,1,0:T(8,128)S(1)} collective-permute-done((f32[4,512,128]{2,1,0:T(8,128)S(1)}, f32[4,512,128]{2,1,0:T(8,128)S(1)}, u32[]{:S(2)}, u32[]{:S(2)}) %collective-permute-start.5) | collective-permute-done | bytes 1048608 | tf_op jit(solution)/shard_map/ppermute | solution.py:245
  132.4 5.5 %shard_map.21 = (bf16[512,1024]{1,0:T(8,128)(2,1)S(1)}, f32[1,512]{1,0:T(1,128)S(1)}, f32[1,512]{1,0:T(1,128)S(1)}) custom-call(f32[4,512,128]{2,1,0:T(8,128)S(1)} %collective-permute-done.4.above_ref, f32[4,512,128]{2,1,0:T(8,128)S(1)} %collective-permute-done.5.below_ref, f32[4,512,128]{2,1,0:T(8,128)S(1)} %get-tuple-element.25.top_ref, ...), custom_call_target="tpu_custom_call" | custom-call | tf_op jit(solution)/shard_map/pallas_call | solution.py:251
  138.0 3.9 %shard_map.22 = (f32[16,35,8,128]{3,2,1,0:T(8,128)S(1)}, f32[16,35,8,128]{3,2,1,0:T(8,128)}) custom-call(bf16[512,1024]{1,0:T(8,128)(2,1)S(1)} %get-tuple-element.23.u0_ref, bf16[512,1024]{1,0:T(8,128)(2,1)S(1)} %get-tuple-element.26.u1_ref, f32[8,128]{1,0:T(8,128)S(1)} %bitcast.6, f32[8,128]{1,0:T(8,128)S(1)} %bitcast.7), custom_call_target="tpu_custom_call" | custom-call | tf_op jit(solution)/shard_map/pallas_call | solution.py:269
  141.9 0.1 collective-permute-start.6
  142.0 4.5 %collective-permute-done.6 = f32[16,35,8,128]{3,2,1,0:T(8,128)S(1)} collective-permute-done((f32[16,35,8,128]{3,2,1,0:T(8,128)}, f32[16,35,8,128]{3,2,1,0:T(8,128)S(1)}, u32[]{:S(2)}, u32[]{:S(2)}) %collective-permute-start.6) | collective-permute-done | bytes 2293792 | tf_op jit(solution)/shard_map/ppermute | solution.py:278
  146.5 0.3 add.3
  146.9 38.9 %all_to_all.10.part_ref = f32[16,35,8,128]{3,2,1,0:T(8,128)S(1)} all-to-all(f32[16,35,8,128]{3,2,1,0:T(8,128)S(1)} %add.3), channel_id=1, replica_groups=mesh['x'=4,'zl'=4,'y'=4,'zh'=2,'c'=2] {'x','y'}, dimensions={0} | all-to-all | bytes 4587520 | tf_op jit(solution)/shard_map/all_to_all | solution.py:279
  185.8 0.6 shard_map.23
  186.4 16.1 %all_to_all.11.part_ref = f32[8,6,8,128]{3,2,1,0:T(8,128)S(1)} all-to-all(f32[8,6,8,128]{3,2,1,0:T(8,128)S(1)} %shard_map.23), channel_id=1, replica_groups=mesh['x'=4,'zl'=4,'y'=4,'zh'=2,'c'=2] {'zl','zh'}, dimensions={0} | all-to-all | bytes 393216 | tf_op jit(solution)/shard_map/all_to_all | solution.py:288
  202.4 1.0 shard_map.24
  (1 shorter events, 0.0 us)
Async XLA Ops:
  0.0 2.2 %copy-start = (f32[1024,8,128]{2,1,0:T(8,128)S(1)}, f32[1024,8,128]{2,1,0:T(8,128)}, u32[]{:S(2)}) copy-start(f32[1024,8,128]{2,1,0:T(8,128)} %param.1) | copy-start | bytes 12582916
  5.0 3.1 %collective-permute-start = (f32[256,128]{1,0:T(8,128)S(1)}, f32[256,128]{1,0:T(8,128)S(1)}, u32[]{:S(2)}, u32[]{:S(2)}) collective-permute-start(f32[256,128]{1,0:T(8,128)S(1)} %get-tuple-element.19), channel_id=1, source_target_pairs={{0,1},{1,2},{2,3},{3,4},{4,5},{5,6},{6,7},{7,8},{8,9},{9,10},{10,1... | collective-permute-start | bytes 393224 | tf_op jit(solution)/shard_map/ppermute | solution.py:224
  6.8 9.3 %collective-permute-start.1 = (f32[256,128]{1,0:T(8,128)S(1)}, f32[256,128]{1,0:T(8,128)S(1)}, u32[]{:S(2)}, u32[]{:S(2)}) collective-permute-start(f32[256,128]{1,0:T(8,128)S(1)} %get-tuple-element.20), channel_id=1, source_target_pairs={{1,0},{2,1},{3,2},{4,3},{5,4},{6,5},{7,6},{8,7},{9,8},{10,9},{11,1... | collective-permute-start | bytes 393224 | tf_op jit(solution)/shard_map/ppermute | solution.py:225
  34.9 30.7 %collective-permute-start.2 = (f32[4,512,128]{2,1,0:T(8,128)S(1)}, f32[4,512,128]{2,1,0:T(8,128)S(1)}, u32[]{:S(2)}, u32[]{:S(2)}) collective-permute-start(f32[4,512,128]{2,1,0:T(8,128)S(1)} %get-tuple-element.21.bot_ref), channel_id=1, source_target_pairs={{0,16},{16,32},{32,48},{48,64},{64,80},{80,96},{96,112},{112,128},... | collective-permute-start | bytes 3145736 | tf_op jit(solution)/shard_map/ppermute | solution.py:245
  37.8 56.1 %collective-permute-start.3 = (f32[4,512,128]{2,1,0:T(8,128)S(1)}, f32[4,512,128]{2,1,0:T(8,128)S(1)}, u32[]{:S(2)}, u32[]{:S(2)}) collective-permute-start(f32[4,512,128]{2,1,0:T(8,128)S(1)} %get-tuple-element.22.top_ref.order_ref), channel_id=1, source_target_pairs={{16,0},{32,16},{48,32},{64,48},{80,64},{96,80},{112,96},{128,112},... | collective-permute-start | bytes 3145736 | tf_op jit(solution)/shard_map/ppermute | solution.py:245
  59.7 39.8 %collective-permute-start.4 = (f32[4,512,128]{2,1,0:T(8,128)S(1)}, f32[4,512,128]{2,1,0:T(8,128)S(1)}, u32[]{:S(2)}, u32[]{:S(2)}) collective-permute-start(f32[4,512,128]{2,1,0:T(8,128)S(1)} %get-tuple-element.24.bot_ref), channel_id=1, source_target_pairs={{0,16},{16,32},{32,48},{48,64},{64,80},{80,96},{96,112},{112,128},... | collective-permute-start | bytes 3145736 | tf_op jit(solution)/shard_map/ppermute | solution.py:245
  62.5 69.9 %collective-permute-start.5 = (f32[4,512,128]{2,1,0:T(8,128)S(1)}, f32[4,512,128]{2,1,0:T(8,128)S(1)}, u32[]{:S(2)}, u32[]{:S(2)}) collective-permute-start(f32[4,512,128]{2,1,0:T(8,128)S(1)} %get-tuple-element.25.top_ref), channel_id=1, source_target_pairs={{16,0},{32,16},{48,32},{64,48},{80,64},{96,80},{112,96},{128,112},... | collective-permute-start | bytes 3145736 | tf_op jit(solution)/shard_map/ppermute | solution.py:245
  141.9 4.7 %collective-permute-start.6 = (f32[16,35,8,128]{3,2,1,0:T(8,128)}, f32[16,35,8,128]{3,2,1,0:T(8,128)S(1)}, u32[]{:S(2)}, u32[]{:S(2)}) collective-permute-start(f32[16,35,8,128]{3,2,1,0:T(8,128)} %get-tuple-element.32), channel_id=1, source_target_pairs={{0,1},{1,0},{2,3},{3,2},{4,5},{5,4},{6,7},{7,6},{8,9},{9,8},{10,11... | collective-permute-start | bytes 6881288 | tf_op jit(solution)/shard_map/ppermute | solution.py:278
